TPU v7x, 256 devices: a whole 4x4x8 slice. The times are simulated.
256 devices in a mesh: dp: 64 (over z_lo, y, x), tensor: 4 (over z_hi, core).
Axes of the slice: x: 4, y: 4, z: 8 (z_hi: 2, z_lo: 4; z = z_hi * 4 + z_lo), core: 2. Of those that a mesh axis runs over, the one named last changes fastest.
Arguments:
- teacher_partial: bfloat16 [4, 16384, 8192], P('tensor', 'dp'), may hold values from -6 to 6
- teacher_resid: bfloat16 [16384, 8192], P('dp'), may hold values from -400 to 400
- norm_gain: float32 [8192], P('tensor'), may hold values from 0.1 to 1.9
- projector: bfloat16 [2048, 8192], P('dp', 'tensor'), may hold values from -0.0625 to 0.0625
- student_hidden: bfloat16 [16384, 2048], P('dp'), may hold values from -6 to 6
Outputs:
- distill_error: bfloat16 [16384, 2048], P(('dp', 'tensor'))
- projector_grad: float32 [2048, 8192], P('dp', 'tensor')
All inputs are finite; a program needn't handle non-finite values.
Results may differ from a plain program's by a relative error of at most 0.015.
Values may be sent and summed in bfloat16 or wider, within the bound.
A program may use at most 128 MiB of HBM per device.

v0:
```python
import jax
import jax.numpy as jnp
from jax import lax
from jax.sharding import PartitionSpec as P

DT = 8192
TOK_DEV = 256


epsilon = 1e-05


def body(teacher_partial, teacher_resid, norm_gain, projector, student_hidden):
    row_count = teacher_resid.shape[0]
    quarter = norm_gain.shape[0]
    tensor_size = lax.axis_size("tensor")
    tensor_index = lax.axis_index("tensor")
    part_rows = row_count // tensor_size
    partial_value = teacher_partial[0]
    summed = lax.psum(partial_value, "tensor").astype(jnp.float32)
    whole = summed + teacher_resid.astype(jnp.float32)
    total_sq = jnp.sum(whole * whole, axis=1)
    hidden = lax.dynamic_slice_in_dim(whole, tensor_index * quarter, quarter, 1)
    inv_rms = lax.rsqrt(total_sq / DT + epsilon)
    normed = (hidden * inv_rms[:, None] * norm_gain[None, :]).astype(jnp.bfloat16)
    partial_proj = lax.dot_general(
        normed,
        lax.all_gather(projector, "dp", axis=0, tiled=True),
        (((1,), (1,)), ((), ())),
        preferred_element_type=jnp.float32,
    )
    summed_proj = lax.psum(partial_proj.astype(jnp.bfloat16), "tensor").astype(jnp.float32)
    error_all = (summed_proj - student_hidden.astype(jnp.float32)).astype(jnp.bfloat16)
    error_part = lax.dynamic_slice_in_dim(error_all, tensor_index * part_rows, part_rows, 0)
    product = lax.dot_general(
        error_all, normed, (((0,), (0,)), ((), ())), preferred_element_type=jnp.float32
    )
    gradient = lax.psum_scatter(product * (1.0 / TOK_DEV), "dp", scatter_dimension=0, tiled=True)
    return (error_part, gradient)


def solution(mesh):
    placed = (P("tensor", "dp", None), P("dp", None), P("tensor"), P("dp", "tensor"), P("dp", None))
    return jax.shard_map(
        body,
        mesh=mesh,
        in_specs=placed,
        out_specs=(P(("dp", "tensor"), None), P("dp", "tensor")),
        check_vma=False,
    )
```

profile of v0, /device:TPU:8, one launch (start us, length us, event | category | flops | bytes accessed | tf_op | source)
XLA Modules:
  0.0 964.6 jit_solution(526644932555769206)
XLA Ops:
  8.0 0.0 all-reduce.3.cloned.1.call-start
  8.0 0.7 all-reduce.3.cloned.1.call-update
  8.7 0.0 all-gather.2.cloned.1.call-start
  8.8 0.5 all-gather.2.cloned.1.call-update
  9.3 0.0 all-reduce.5.cloned.1.call-start
  9.4 0.0 copy-start.1
  9.4 180.7 %all-reduce.3.cloned.1.call-done = bf16[256,8192]{1,0:T(8,128)(2,1)} async-done(((bf16[256,8192]{1,0:T(8,128)(2,1)}), bf16[256,8192]{1,0:T(8,128)(2,1)}) %all-reduce.3.cloned.1.call-update) | async-done | bytes 4194320 | tf_op jit(solution)/shard_map/psum | solution.py:20
  190.1 8.0 multiply_reduce_fusion
  198.1 269.0 %all-gather.2.cloned.1.call-done = bf16[2048,2048]{1,0:T(8,128)(2,1)} async-done(((bf16[32,2048]{1,0:T(8,128)(2,1)}), bf16[2048,2048]{1,0:T(8,128)(2,1)}) %all-gather.2.cloned.1.call-update) | async-done | bytes 8388624 | tf_op jit(solution)/shard_map/all_gather | solution.py:28
  467.1 0.0 copy-done.1
  467.1 0.0 copy-start
  467.1 7.5 convolution_convert_fusion
  474.6 0.0 all-reduce.5.cloned.1.call-update
  474.6 0.0 reduce-scatter.2.cloned.1.call-start
  474.7 74.2 %all-reduce.5.cloned.1.call-done = bf16[256,2048]{1,0:T(8,128)(2,1)} async-done(((bf16[256,2048]{1,0:T(8,128)(2,1)}), bf16[256,2048]{1,0:T(8,128)(2,1)}) %all-reduce.5.cloned.1.call-update) | async-done | bytes 1048592 | tf_op jit(solution)/shard_map/psum | solution.py:32
  548.9 0.0 copy-done
  548.9 1.6 subtract_convert_fusion
  550.5 9.8 %convolution_multiply_fusion = f32[2048,2048]{1,0:T(8,128)} fusion(bf16[256,2048]{1,0:T(8,128)(2,1)S(1)} %subtract_convert_fusion, f32[256,8192]{1,0:T(8,128)} %get-tuple-element.3, s32[]{:T(128)S(6)} %select_n.6, f32[2048]{0:T(1024)S(1)} %copy-done.1, f32[256]{0:T(256)S(1)} %add_rsqrt_fusion), kind=kOutput, calls=%fused_computation | convolution fusion | flops 2153250816 | bytes 19932164 | tf_op jit(solution)/shard_map/dot_general | solution.py:35
  560.3 0.0 reduce-scatter.2.cloned.1.call-update
  560.3 0.7 constant_dynamic-slice_fusion
  561.1 396.1 %reduce-scatter.2.cloned.1.call-done = f32[32,2048]{1,0:T(8,128)} async-done(((f32[2048,2048]{1,0:T(8,128)}), f32[32,2048]{1,0:T(8,128)}) %reduce-scatter.2.cloned.1.call-update) | async-done | bytes 262160 | tf_op jit(solution)/shard_map/reduce_scatter | solution.py:38
  (1 shorter events, 0.0 us)
Async XLA Ops:
  8.0 182.1 %all-reduce.3.cloned.1.call-start = ((), (), s32[]{:S(2)}) async-start(), calls=%async_computation.1 | async-start | bytes 8388608 | tf_op jit(solution)/shard_map/psum | solution.py:20
  8.7 458.3 %all-gather.2.cloned.1.call-start = ((), (), s32[]{:S(2)}) async-start(), calls=%async_computation.2 | async-start | bytes 8519680 | tf_op jit(solution)/shard_map/all_gather | solution.py:28
  9.3 539.6 %all-reduce.5.cloned.1.call-start = ((), (), s32[]{:S(2)}) async-start(), calls=%async_computation.3 | async-start | bytes 2097152 | tf_op jit(solution)/shard_map/psum | solution.py:32
  9.4 457.7 %copy-start.1 = (f32[2048]{0:T(1024)S(1)}, f32[2048]{0:T(1024)}, u32[]{:S(2)}) copy-start(f32[2048]{0:T(1024)} %param.7) | copy-start | bytes 24580
  467.1 81.8 %copy-start = (bf16[256,2048]{1,0:T(8,128)(2,1)S(1)}, bf16[256,2048]{1,0:T(8,128)(2,1)}, u32[]{:S(2)}) copy-start(bf16[256,2048]{1,0:T(8,128)(2,1)} %param.9) | copy-start | bytes 3145732
  474.6 482.5 %reduce-scatter.2.cloned.1.call-start = ((), (), s32[]{:S(2)}) async-start(), calls=%async_computation.4 | async-start | bytes 17039360 | tf_op jit(solution)/shard_map/reduce_scatter | solution.py:38
Sparse Core Ops, SparseCore 0:
  11.5 178.5 all-reduce.2
  474.7 74.1 all-reduce.4
Sparse Core Ops, SparseCore 1:
  11.1 455.9 all-gather.1
  560.4 396.6 reduce-scatter.1
where the time goes:
time: 975 us; the launch traced here: 965 us
  waiting for transfers between devices  921 us (94%)
  matrix products  17.3 us (2%)
  between operations  15.5 us (2%)
    reduce_scatter x1, waiting for transfers between devices, body(): lax.psum_scatter(product * (1.0 / TOK_DEV), 'dp', scatter_dimension=0, ti...  396 us
    all_gather x1, waiting for transfers between devices, body(): lax.all_gather(projector, 'dp', axis=0, tiled=True)  269 us
    psum x1, waiting for transfers between devices, body(): summed = lax.psum(partial_value, 'tensor').astype(jnp.float32)  181 us
    psum x1, waiting for transfers between devices, body(): lax.psum(partial_proj.astype(jnp.bfloat16), 'tensor').astype(jnp.float32)  74.2 us
  transfers between devices with their start and end apart: 4, of which 4 were waited for; matrix products, arithmetic and copies ran while one was open for 1% of the time, Pallas kernels for 0%

commit v1 on v0

v1 whole, which is shorter than its diff:
```python
import jax
import jax.numpy as jnp
from jax import lax
from jax.experimental import pallas as pl
from jax.experimental.pallas import tpu as pltpu
from jax.sharding import PartitionSpec as P

MESH_ID = pl.DeviceIdType.MESH
F32 = jnp.float32
BF16 = jnp.bfloat16
EPS = 1e-05
DT = 8192
NX_, NY_, NZL, NZ = 4, 4, 4, 8
K = 4
TILE = 512


def dot_nt(a, b):
    return lax.dot_general(a, b, (((1,), (1,)), ((), ())), preferred_element_type=F32)


def dot_tn(a, b):
    return lax.dot_general(a, b, (((0,), (0,)), ((), ())), preferred_element_type=F32)


def kernel(
    tp, res, gain, proj, stu, out_e, out_g,
    t_own, t_rem, r_own, hid, z_out, z_in, gains, sq_out, sq_in, n_out, norm,
    w, st_raw, st_out, st_in, pp, pp_out, pp_in, q_out, q_in, err, e_in, grad, g_out, g_in, f_out, f_in,
    send_sem, recv_sem, local_sem,
):
    dp = lax.axis_index("dp")
    tensor = lax.axis_index("tensor")
    x = lax.rem(dp, NX_)
    y = lax.rem(dp // NX_, NY_)
    zl = dp // (NX_ * NY_)
    zh = tensor // 2
    c = lax.rem(tensor, 2)
    z = zh * NZL + zl
    other = 1 - c

    def device(dx=0, dy=0, dz=0, dc=0):
        x1 = lax.rem(x + dx, NX_)
        y1 = lax.rem(y + dy, NY_)
        z1 = lax.rem(z + dz, NZ)
        c1 = lax.rem(c + dc, 2)
        return (lax.rem(z1, NZL) * (NX_ * NY_) + y1 * NX_ + x1, (z1 // NZL) * 2 + c1)

    counts = {"remote": 0, "local": 0}
    sends = []

    def remote(src, dst, **offset):
        i = counts["remote"]
        counts["remote"] += 1
        copy = pltpu.make_async_remote_copy(
            src, dst, send_sem.at[i], recv_sem.at[i], device_id=device(**offset), device_id_type=MESH_ID
        )
        copy.start()
        sends.append(copy)
        return copy

    def local(src, dst):
        i = counts["local"]
        counts["local"] += 1
        copy = pltpu.make_async_copy(src, dst, local_sem.at[i])
        copy.start()
        return copy

    def cols(index, width):
        return pl.ds(pl.multiple_of(index * width, width), width)

    early = [
        [local(tp.at[1 - zh, :, k, :, cols(2 * h + c, 2048)], t_own.at[0, :, k, :, pl.ds(h * 2048, 2048)]) for h in range(2)]
        for k in range(K)
    ]
    late = [local(tp.at[zh, :, :, :, cols(2 * h + c, 2048)], t_own.at[1, :, :, :, pl.ds(h * 2048, 2048)]) for h in range(2)]
    late += [local(res.at[zh, :, :, :, cols(2 * h + c, 2048)], r_own.at[:, :, :, pl.ds(h * 2048, 2048)]) for h in range(2)]
    late_gain = local(gain, gains.at[zh])
    late_student = local(stu.at[zh, c], st_raw)
    late_w = local(proj.at[:, cols(x, TILE)], w.at[z, pl.ds(pl.multiple_of(x * 32, 32), 32)])

    partners = [dict(dc=1)]
    partners += [dict(dz=d) for d in range(1, NZ)]
    partners += [dict(dx=d, dc=e) for d in range(1, NX_) for e in range(2)]
    partners += [dict(dy=d) for d in range(1, NY_)]
    barrier = pltpu.get_barrier_semaphore()
    for offset in partners:
        pl.semaphore_signal(barrier, inc=1, device_id=device(**offset), device_id_type=MESH_ID)
    pl.semaphore_wait(barrier, len(partners))

    early_in = [
        [
            remote(tp.at[1 - zh, :, k, :, cols(2 * h + other, 2048)], t_rem.at[0, :, k, :, pl.ds(h * 2048, 2048)], dc=1)
            for h in range(2)
        ]
        for k in range(K)
    ]
    late_in = [
        remote(tp.at[zh, :, :, :, cols(2 * h + other, 2048)], t_rem.at[1, :, :, :, pl.ds(h * 2048, 2048)], dc=1)
        for h in range(2)
    ]
    w_x = [
        remote(proj.at[:, cols(lax.rem(x + d, NX_), TILE)], w.at[z, pl.ds(pl.multiple_of(x * 32, 32), 32)], dx=d)
        for d in range(1, NX_)
    ]

    z_copy = []
    for k in range(K):
        for h in range(2):
            early[k][h].wait()
            early_in[k][h].wait_recv()

        @pl.loop(0, 4096 // TILE)
        def _(t, k=k):
            at = cols(t, TILE)
            pair = t_own[0, :, k, :, at].astype(F32) + t_rem[0, :, k, :, at].astype(F32)
            z_out[k, :, :, at] = pair.astype(BF16)

        z_copy.append(remote(z_out.at[k], z_in.at[k], dz=4))

    late_w.wait()
    for copy in w_x:
        copy.wait_recv()

    def ring_step(s):
        right = lax.rem(z + NZ - (s - 1), NZ)
        left = lax.rem(z + (s - 1), NZ)
        copies = [remote(w.at[right], w.at[right], dz=1)]
        if s < 4:
            copies.append(remote(w.at[left], w.at[left], dz=NZ - 1))
        return copies

    ring = ring_step(1)
    gain_in = remote(gain, gains.at[zh], dz=4)

    for copy in late:
        copy.wait()
    for copy in late_in:
        copy.wait_recv()
    for k in range(K):

        @pl.loop(0, 4096 // TILE)
        def _(t, k=k):
            at = cols(t, TILE)
            hid[k, :, :, at] = (
                r_own[:, k, :, at].astype(F32) + t_own[1, :, k, :, at].astype(F32) + t_rem[1, :, k, :, at].astype(F32)
            )

    late_student.wait()
    for y1 in range(NY_):
        for b in range(NZL):
            st_out[y1, :, :, b * 128 : (b + 1) * 128] = st_raw[:, :, b * 512 + y1 * 128 : b * 512 + (y1 + 1) * 128]
    st_own = local(st_out.at[y], st_in.at[y])
    st_copy = [remote(st_out.at[lax.rem(y + d, NY_)], st_in.at[y], dy=d) for d in range(1, NY_)]

    for copy in ring:
        copy.wait_recv()
    ring = ring_step(2)
    late_gain.wait()
    gain_in.wait_recv()

    x_copy, y_copy, p_copy, q_copy, e_copy, o_copy = {}, {}, {}, {}, {}, {}

    def normalise(k):
        z_copy[k].wait_recv()

        def add(t, total):
            at = cols(t, TILE)
            value = hid[k, :, :, at] + z_in[k, :, :, at].astype(F32)
            hid[k, :, :, at] = value
            square = value * value
            for b in range(TILE // 128):
                total = total + square[:, :, b * 128 : (b + 1) * 128]
            return total

        total = lax.fori_loop(0, 4096 // TILE, add, jnp.zeros((2, 16, 128), F32))
        sq_out[k] = total
        copy = remote(sq_out.at[k], sq_in.at[k], dc=1)
        copy.wait_recv()
        whole = jnp.sum(sq_out[k] + sq_in[k], axis=-1, keepdims=True)
        inv = lax.rsqrt(whole / DT + EPS)
        for h in range(2):

            @pl.loop(0, NX_)
            def _(x1, h=h):
                at = pl.ds(pl.multiple_of(h * 2048 + x1 * TILE, TILE), TILE)
                g = gains[h, :, cols(x1, TILE)]
                n_out[k, x1, :, :, h * TILE : (h + 1) * TILE] = (hid[k, :, :, at] * inv * g[None]).astype(BF16)

        x_copy[k] = [local(n_out.at[k, x], norm.at[k, y, x])]
        x_copy[k] += [remote(n_out.at[k, lax.rem(x + d, NX_)], norm.at[k, y, x], dx=d) for d in range(1, NX_)]

    def gather_y(k):
        x_copy[k][0].wait()
        for copy in x_copy[k][1:]:
            copy.wait_recv()
        y_copy[k] = [remote(norm.at[k, y], norm.at[k, y], dy=d) for d in range(1, NY_)]

    def project(k):
        for copy in y_copy[k]:
            copy.wait_recv()
        for mine in (False, True):
            half = c if mine else other
            for n in range(2):
                total = None
                for h in range(2):
                    rows = norm[k, :, :, half, :, h * TILE : (h + 1) * TILE].reshape(256, TILE)
                    weights = w[4 * h + 2 * n : 4 * h + 2 * n + 2].reshape(256, TILE)
                    part = dot_nt(rows, weights)
                    total = part if total is None else total + part
                total = total.reshape(NY_, NX_, 16, 256)
                if mine:
                    pp[:, :, :, n * 256 : (n + 1) * 256] = total
                else:
                    pp_out[k, :, :, :, n * 256 : (n + 1) * 256] = total.astype(BF16)
            if not mine:
                p_copy[k] = remote(pp_out.at[k], pp_in.at[k], dc=1)

    def pair_up(k):
        p_copy[k].wait_recv()

        @pl.loop(0, NY_)
        def _(y1):
            total = pp[y1] + pp_in[k, y1].astype(F32)
            pp[y1] = total
            q_out[k, y1] = total.astype(BF16)

        q_copy[k] = [remote(q_out.at[k, :, lax.rem(x + d, NX_)], q_in.at[k, x], dx=d) for d in range(1, NX_)]

    def subtract(k):
        for copy in q_copy[k]:
            copy.wait_recv()

        @pl.loop(0, NY_)
        def _(y1):
            total = pp[y1, x]
            for d in range(1, NX_):
                total = total + q_in[k, lax.rem(x + d, NX_), y1].astype(F32)
            err[k, y1, x, c] = (total - st_in[y1, k].astype(F32)).astype(BF16)

        e_copy[k] = [
            remote(err.at[k, :, x, c], err.at[k, :, x, c], dx=d, dc=e)
            for d in range(NX_) for e in range(2) if (d, e) != (0, 0)
        ]
        e_in[y, k] = err[k, y, x, c]
        o_copy[k] = [remote(err.at[k, lax.rem(y + d, NY_), x, c], e_in.at[y, k], dy=d) for d in range(1, NY_)]

    def accumulate(k):
        for copy in e_copy[k]:
            copy.wait_recv()
        e = err[k].reshape(512, 512)
        for h in range(2):
            n = norm[k, :, :, :, :, h * TILE : (h + 1) * TILE].reshape(512, TILE)
            part = dot_tn(e, n).reshape(NZL, 128, TILE)
            grad[h] = part if k == 0 else grad[h] + part

    for copy in st_copy:
        copy.wait_recv()
    st_own.wait()

    for k in range(K + 1):
        if k < K:
            normalise(k)
        if k == 0 or k == 1:
            for copy in ring:
                copy.wait_recv()
            ring = ring_step(3 + k)
        if k == 1:
            for copy in ring:
                copy.wait_recv()
        if k >= 1:
            project(k - 1)
        if k < K:
            gather_y(k)
        if k >= 1:
            pair_up(k - 1)
        if k >= 2:
            accumulate(k - 2)
        if k >= 1:
            subtract(k - 1)
    accumulate(K - 1)

    for h in range(2):
        for b in range(NZL):
            g_out[h * NZL + b] = grad[h, b].astype(BF16)
    g_copy = [remote(g_out.at[lax.rem(z + d, NZ)], g_in.at[z], dz=d) for d in range(1, NZ)]
    for k in range(K):
        for copy in o_copy[k]:
            copy.wait_recv()
    for y1 in range(NY_):
        for b in range(NZL):
            out_e[:, :, b * 512 + y1 * 128 : b * 512 + (y1 + 1) * 128] = e_in[y1, :, :, b * 128 : (b + 1) * 128]
    for copy in g_copy:
        copy.wait_recv()

    @pl.loop(0, NX_)
    def _(x1):
        at = pl.ds(pl.multiple_of(x1 * 32, 32), 32)
        total = grad[zh, zl, at]
        for d in range(1, NZ):
            total = total + g_in[lax.rem(z + d, NZ), at].astype(F32)
        f_out[x1] = total * (1.0 / 256)

    f_in[x] = f_out[x]
    f_copy = [remote(f_out.at[lax.rem(x + d, NX_)], f_in.at[x], dx=d) for d in range(1, NX_)]
    for copy in f_copy:
        copy.wait_recv()
    for x1 in range(NX_):
        out_g[:, x1 * TILE : (x1 + 1) * TILE] = f_in[x1]
    for copy in sends:
        copy.wait_send()


def body(teacher_partial, teacher_resid, norm_gain, projector, student_hidden):
    tp = teacher_partial.reshape(2, 2, K, 16, DT)
    res = teacher_resid.reshape(2, 2, K, 16, DT)
    stu = student_hidden.reshape(2, 2, K, 16, 2048)
    hbm = pl.BlockSpec(memory_space=pl.ANY)
    vmem = pl.BlockSpec(memory_space=pltpu.VMEM)
    error, gradient = pl.pallas_call(
        kernel,
        out_shape=(jax.ShapeDtypeStruct((K, 16, 2048), BF16), jax.ShapeDtypeStruct((32, 2048), F32)),
        in_specs=[hbm] * 5,
        out_specs=(vmem, vmem),
        scratch_shapes=[
            pltpu.VMEM((2, 2, K, 16, 4096), BF16),
            pltpu.VMEM((2, 2, K, 16, 4096), BF16),
            pltpu.VMEM((2, K, 16, 4096), BF16),
            pltpu.VMEM((K, 2, 16, 4096), F32),
            pltpu.VMEM((K, 2, 16, 4096), BF16),
            pltpu.VMEM((K, 2, 16, 4096), BF16),
            pltpu.VMEM((2, 1, 2048), F32),
            pltpu.VMEM((K, 2, 16, 128), F32),
            pltpu.VMEM((K, 2, 16, 128), F32),
            pltpu.VMEM((K, 4, 2, 16, 1024), BF16),
            pltpu.VMEM((K, 4, 4, 2, 16, 1024), BF16),
            pltpu.VMEM((8, 128, 512), BF16),
            pltpu.VMEM((K, 16, 2048), BF16),
            pltpu.VMEM((4, K, 16, 512), BF16),
            pltpu.VMEM((4, K, 16, 512), BF16),
            pltpu.VMEM((4, 4, 16, 512), F32),
            pltpu.VMEM((K, 4, 4, 16, 512), BF16),
            pltpu.VMEM((K, 4, 4, 16, 512), BF16),
            pltpu.VMEM((K, 4, 4, 16, 512), BF16),
            pltpu.VMEM((K, 4, 4, 16, 512), BF16),
            pltpu.VMEM((K, 4, 4, 2, 16, 512), BF16),
            pltpu.VMEM((4, K, 16, 512), BF16),
            pltpu.VMEM((2, 4, 128, 512), F32),
            pltpu.VMEM((8, 128, 512), BF16),
            pltpu.VMEM((8, 128, 512), BF16),
            pltpu.VMEM((4, 32, 512), F32),
            pltpu.VMEM((4, 32, 512), F32),
            pltpu.SemaphoreType.DMA((128,)),
            pltpu.SemaphoreType.DMA((128,)),
            pltpu.SemaphoreType.DMA((32,)),
        ],
        compiler_params=pltpu.CompilerParams(
            collective_id=0, has_side_effects=True, vmem_limit_bytes=56 << 20
        ),
        name="distill",
    )(tp, res, norm_gain.reshape(1, -1), projector, stu)
    return error.reshape(-1, 2048), gradient


def solution(mesh):
    placed = (P("tensor", "dp", None), P("dp", None), P("tensor"), P("dp", "tensor"), P("dp", None))
    return jax.shard_map(
        body,
        mesh=mesh,
        in_specs=placed,
        out_specs=(P(("dp", "tensor"), None), P("dp", "tensor")),
        check_vma=False,
    )
```

time: 975 us -> 184 us (0.19)
  waiting for transfers between devices: 921 us -> 0 us
  Pallas kernels: 0 us -> 178 us
  matrix products: 17.3 us -> 0 us
  between operations: 15.5 us -> 0.64 us
    reduce_scatter x1 -> x0, waiting for transfers between devices: 396 us -> none  [body(): lax.psum_scatter(product * (1.0 / TOK_DEV), 'dp', scatter_dimension=0, ti...]
    all_gather x1 -> x0, waiting for transfers between devices: 269 us -> none  [body(): lax.all_gather(projector, 'dp', axis=0, tiled=True)]
    psum x2 -> x0, waiting for transfers between devices: 255 us -> none  [the longest x1 181 us: body(): summed = lax.psum(partial_value, 'tensor').astype(jnp.float32)]
    pallas_call x0 -> x1, Pallas kernels: none -> 178 us  [body(): pl.pallas_call(kernel, out_shape=(jax.ShapeDtypeStruct((K, 16, 2048), BF1...]
    dot_general x2 -> x0, matrix products: 17.3 us -> none  [the longest x1 9.79 us: body(): lax.dot_general(error_all, normed, (((0,), (0,)), ((), ())), preferred_el...]
  transfers between devices with their start and end apart: 4 -> 0, of which waited for: 4 -> 0; matrix products, arithmetic and copies ran while one was open for 1% -> 0% of each run, Pallas kernels for 0% -> 0%
where the time goes in v1:
time: 184 us; the launch traced here: 182 us
  Pallas kernels  178 us (97%)
  local copies, waits for them, and re-layouts  3.34 us (2%)
    pallas_call x1, Pallas kernels, body(): pl.pallas_call(kernel, out_shape=(jax.ShapeDtypeStruct((K, 16, 2048), BF1...  178 us

profile of v1, /device:TPU:8, one launch (start us, length us, event | category | flops | bytes accessed | tf_op | source)
XLA Modules:
  0.0 182.1 jit_solution(13415695466746767424)
XLA Ops:
  0.6 178.2 %distill.1 = (bf16[4,16,2048]{2,1,0:T(8,128)(2,1)}, f32[32,2048]{1,0:T(8,128)}) custom-call(bf16[2,2,4,16,8192]{4,3,2,1,0:T(8,128)(2,1)} %bitcast.5, bf16[2,2,4,16,8192]{4,3,2,1,0:T(8,128)(2,1)} %bitcast.6, f32[1,2048]{1,0:T(1,128)} %bitcast.9, bf16[32,2048]{1,0:T(8,128)(2,1)} %proj.1, bf16[2,2,4,16,2048]{4,3,2,1,0:T(8,128)(2,1)} %bitcast.7), custom_call_target="tpu_custom_call" | custom-call | tf_op jit(solution)/shard_map/distill/pallas_call | solution.py:320
  178.8 1.7 copy.9
  180.5 1.7 copy.10

commit v2 on v1

--- a/solution.py
+++ b/solution.py
@@ -27,7 +27,7 @@
     tp, res, gain, proj, stu, out_e, out_g,
     t_own, t_rem, r_own, hid, z_out, z_in, gains, sq_out, sq_in, n_out, norm,
     w, st_raw, st_out, st_in, pp, pp_out, pp_in, q_out, q_in, err, e_in, grad, g_out, g_in, f_out, f_in,
-    send_sem, recv_sem, local_sem,
+    send_sem, recv_sem, local_sem, ready,
 ):
     dp = lax.axis_index("dp")
     tensor = lax.axis_index("tensor")
@@ -81,13 +81,14 @@
 
     partners = [dict(dc=1)]
     partners += [dict(dz=d) for d in range(1, NZ)]
-    partners += [dict(dx=d, dc=e) for d in range(1, NX_) for e in range(2)]
+    partners += [dict(dx=d) for d in range(1, NX_)]
     partners += [dict(dy=d) for d in range(1, NY_)]
     barrier = pltpu.get_barrier_semaphore()
     for offset in partners:
         pl.semaphore_signal(barrier, inc=1, device_id=device(**offset), device_id_type=MESH_ID)
     pl.semaphore_wait(barrier, len(partners))
 
+    gain_in = remote(gain, gains.at[zh], dz=4)
     early_in = [
         [
             remote(tp.at[1 - zh, :, k, :, cols(2 * h + other, 2048)], t_rem.at[0, :, k, :, pl.ds(h * 2048, 2048)], dc=1)
@@ -104,39 +105,46 @@
         for d in range(1, NX_)
     ]
 
-    z_copy = []
-    for k in range(K):
+    pieces = [(k, half, h) for k in range(K) for half in range(2) for h in range(2)]
+    z_copy = {}
+
+    def send_pieces(first, last):
+        for k, half, h in pieces[first:last]:
+            at = pl.ds(h * 2048, 2048)
+            z_copy[k, half, h] = remote(z_out.at[k, half, :, at], z_in.at[k, half, :, at], dz=4)
+
+    def ring_step(s):
+        right = lax.rem(z + NZ - (s - 1), NZ)
+        left = lax.rem(z + (s - 1), NZ)
+        return [remote(w.at[right], w.at[right], dz=1), remote(w.at[left], w.at[left], dz=NZ - 1)]
+
+    def arrived(copies):
+        for copy in copies:
+            copy.wait_recv()
+
+    def pair_sum(k):
         for h in range(2):
             early[k][h].wait()
             early_in[k][h].wait_recv()
 
         @pl.loop(0, 4096 // TILE)
-        def _(t, k=k):
+        def _(t):
             at = cols(t, TILE)
             pair = t_own[0, :, k, :, at].astype(F32) + t_rem[0, :, k, :, at].astype(F32)
             z_out[k, :, :, at] = pair.astype(BF16)
 
-        z_copy.append(remote(z_out.at[k], z_in.at[k], dz=4))
-
+    pair_sum(0)
+    send_pieces(0, 2)
+    for k in range(1, K):
+        pair_sum(k)
     late_w.wait()
-    for copy in w_x:
-        copy.wait_recv()
-
-    def ring_step(s):
-        right = lax.rem(z + NZ - (s - 1), NZ)
-        left = lax.rem(z + (s - 1), NZ)
-        copies = [remote(w.at[right], w.at[right], dz=1)]
-        if s < 4:
-            copies.append(remote(w.at[left], w.at[left], dz=NZ - 1))
-        return copies
-
+    arrived(w_x)
     ring = ring_step(1)
-    gain_in = remote(gain, gains.at[zh], dz=4)
+    far = remote(w.at[z], w.at[z], dz=4)
 
     for copy in late:
         copy.wait()
-    for copy in late_in:
-        copy.wait_recv()
+    arrived(late_in)
     for k in range(K):
 
         @pl.loop(0, 4096 // TILE)
@@ -153,16 +161,16 @@
     st_own = local(st_out.at[y], st_in.at[y])
     st_copy = [remote(st_out.at[lax.rem(y + d, NY_)], st_in.at[y], dy=d) for d in range(1, NY_)]
 
-    for copy in ring:
-        copy.wait_recv()
+    arrived(ring)
     ring = ring_step(2)
+    send_pieces(2, 3)
     late_gain.wait()
     gain_in.wait_recv()
 
-    x_copy, y_copy, p_copy, q_copy, e_copy, o_copy = {}, {}, {}, {}, {}, {}
+    x_copy, y_copy, p_copy, q_copy, e_copy, s_copy, o_copy = {}, {}, {}, {}, {}, {}, {}
 
     def normalise(k):
-        z_copy[k].wait_recv()
+        arrived([z_copy[k, half, h] for half in range(2) for h in range(2)])
 
         def add(t, total):
             at = cols(t, TILE)
@@ -194,10 +202,16 @@
         x_copy[k][0].wait()
         for copy in x_copy[k][1:]:
             copy.wait_recv()
-        y_copy[k] = [remote(norm.at[k, y], norm.at[k, y], dy=d) for d in range(1, NY_)]
+        y_copy[k] = [remote(norm.at[k, y], norm.at[k, y], dy=d) for d in (1, NY_ - 1)]
+
+    def forward_y(k):
+        for i, d in enumerate((1, NY_ - 1)):
+            y_copy[k][i].wait_recv()
+            rows = norm.at[k, lax.rem(y + NY_ - d, NY_), 2 * i : 2 * i + 2]
+            y_copy[k].append(remote(rows, rows, dy=d))
 
     def project(k):
-        for copy in y_copy[k]:
+        for copy in y_copy[k][2:]:
             copy.wait_recv()
         for mine in (False, True):
             half = c if mine else other
@@ -238,67 +252,96 @@
                 total = total + q_in[k, lax.rem(x + d, NX_), y1].astype(F32)
             err[k, y1, x, c] = (total - st_in[y1, k].astype(F32)).astype(BF16)
 
-        e_copy[k] = [
-            remote(err.at[k, :, x, c], err.at[k, :, x, c], dx=d, dc=e)
-            for d in range(NX_) for e in range(2) if (d, e) != (0, 0)
-        ]
+        e_copy[k] = [remote(err.at[k, :, x, c], err.at[k, :, x, c], dx=d) for d in range(1, NX_)]
         e_in[y, k] = err[k, y, x, c]
         o_copy[k] = [remote(err.at[k, lax.rem(y + d, NY_), x, c], e_in.at[y, k], dy=d) for d in range(1, NY_)]
 
-    def accumulate(k):
+    def share(k):
         for copy in e_copy[k]:
             copy.wait_recv()
+        s_copy[k] = remote(err.at[k, :, :, c], err.at[k, :, :, c], dc=1)
+
+    def accumulate(k):
+        s_copy[k].wait_recv()
         e = err[k].reshape(512, 512)
         for h in range(2):
             n = norm[k, :, :, :, :, h * TILE : (h + 1) * TILE].reshape(512, TILE)
             part = dot_tn(e, n).reshape(NZL, 128, TILE)
             grad[h] = part if k == 0 else grad[h] + part
 
-    for copy in st_copy:
-        copy.wait_recv()
+    arrived(st_copy)
     st_own.wait()
 
-    for k in range(K + 1):
+    arrived(ring)
+    ring = ring_step(3)
+    send_pieces(3, 4)
+    arrived(ring)
+    arrived([far])
+    send_pieces(4, 6)
+    pl.semaphore_signal(ready.at[0], inc=1, device_id=device(dc=1), device_id_type=MESH_ID)
+    pl.semaphore_wait(ready.at[0], 1)
+    for d in range(1, NZ):
+        pl.semaphore_signal(ready.at[1], inc=1, device_id=device(dz=d), device_id_type=MESH_ID)
+    pl.semaphore_wait(ready.at[1], NZ - 1)
+    send_pieces(6, len(pieces))
+    normalise(0)
+    gather_y(0)
+    forward_y(0)
+    for k in range(1, K + 1):
         if k < K:
             normalise(k)
-        if k == 0 or k == 1:
-            for copy in ring:
-                copy.wait_recv()
-            ring = ring_step(3 + k)
-        if k == 1:
-            for copy in ring:
-                copy.wait_recv()
-        if k >= 1:
-            project(k - 1)
+        if k >= 2:
+            subtract(k - 2)
         if k < K:
             gather_y(k)
-        if k >= 1:
-            pair_up(k - 1)
+        project(k - 1)
         if k >= 2:
+            share(k - 2)
+        pair_up(k - 1)
+        if 2 <= k < K:
             accumulate(k - 2)
-        if k >= 1:
-            subtract(k - 1)
-    accumulate(K - 1)
-
-    for h in range(2):
-        for b in range(NZL):
-            g_out[h * NZL + b] = grad[h, b].astype(BF16)
-    g_copy = [remote(g_out.at[lax.rem(z + d, NZ)], g_in.at[z], dz=d) for d in range(1, NZ)]
-    for k in range(K):
-        for copy in o_copy[k]:
-            copy.wait_recv()
-    for y1 in range(NY_):
-        for b in range(NZL):
-            out_e[:, :, b * 512 + y1 * 128 : b * 512 + (y1 + 1) * 128] = e_in[y1, :, :, b * 128 : (b + 1) * 128]
-    for copy in g_copy:
-        copy.wait_recv()
-
-    @pl.loop(0, NX_)
-    def _(x1):
-        at = pl.ds(pl.multiple_of(x1 * 32, 32), 32)
-        total = grad[zh, zl, at]
-        for d in range(1, NZ):
-            total = total + g_in[lax.rem(z + d, NZ), at].astype(F32)
+        if k < K:
+            forward_y(k)
+    for k in range(K - 1, K + 1):
+        if k == K:
+            subtract(K - 1)
+            share(K - 1)
+        accumulate(k - 1)
+
+    def hops(sub, way):
+        return 4 if sub == way else 3
+
+    g_copy = {}
+    for s in range(1, 5):
+        for sub in range(2):
+            for way in range(2):
+                n = hops(sub, way)
+                if s > n:
+                    continue
+                far = n + 1 - s
+                d = lax.rem(z + (far if way == 0 else NZ - far), NZ)
+                total = grad[d // NZL, lax.rem(d, NZL), sub * 64 : (sub + 1) * 64]
+                if s > 1:
+                    g_copy[sub, way, s - 1].wait_recv()
+                    total = total + g_in[sub, way, s - 2].astype(F32)
+                g_out[sub, way, s - 1] = total.astype(BF16)
+                g_copy[sub, way, s] = remote(
+                    g_out.at[sub, way, s - 1], g_in.at[sub, way, s - 1], dz=1 if way == 0 else NZ - 1
+                )
+        if s == 1:
+            for k in range(K):
+                arrived(o_copy[k])
+            for y1 in range(NY_):
+                for b in range(NZL):
+                    out_e[:, :, b * 512 + y1 * 128 : b * 512 + (y1 + 1) * 128] = e_in[y1, :, :, b * 128 : (b + 1) * 128]
+    for x1 in range(NX_):
+        sub, part = divmod(x1, 2)
+        total = grad[zh, zl, x1 * 32 : (x1 + 1) * 32]
+        for way in range(2):
+            n = hops(sub, way)
+            if part == 0:
+                g_copy[sub, way, n].wait_recv()
+            total = total + g_in[sub, way, n - 1, part * 32 : (part + 1) * 32].astype(F32)
         f_out[x1] = total * (1.0 / 256)
 
     f_in[x] = f_out[x]
@@ -309,6 +352,11 @@
         out_g[:, x1 * TILE : (x1 + 1) * TILE] = f_in[x1]
     for copy in sends:
         copy.wait_send()
+
+
+def place(error, gradient, out_e, out_g):
+    out_e[...] = error[...]
+    out_g[...] = gradient[...]
 
 
 def body(teacher_partial, teacher_resid, norm_gain, projector, student_hidden):
@@ -346,20 +394,27 @@
             pltpu.VMEM((K, 4, 4, 2, 16, 512), BF16),
             pltpu.VMEM((4, K, 16, 512), BF16),
             pltpu.VMEM((2, 4, 128, 512), F32),
-            pltpu.VMEM((8, 128, 512), BF16),
-            pltpu.VMEM((8, 128, 512), BF16),
+            pltpu.VMEM((2, 2, 4, 64, 512), BF16),
+            pltpu.VMEM((2, 2, 4, 64, 512), BF16),
             pltpu.VMEM((4, 32, 512), F32),
             pltpu.VMEM((4, 32, 512), F32),
-            pltpu.SemaphoreType.DMA((128,)),
-            pltpu.SemaphoreType.DMA((128,)),
+            pltpu.SemaphoreType.DMA((160,)),
+            pltpu.SemaphoreType.DMA((160,)),
             pltpu.SemaphoreType.DMA((32,)),
+            pltpu.SemaphoreType.REGULAR((2,)),
         ],
         compiler_params=pltpu.CompilerParams(
             collective_id=0, has_side_effects=True, vmem_limit_bytes=56 << 20
         ),
         name="distill",
     )(tp, res, norm_gain.reshape(1, -1), projector, stu)
-    return error.reshape(-1, 2048), gradient
+    return pl.pallas_call(
+        place,
+        out_shape=(jax.ShapeDtypeStruct((64, 2048), BF16), jax.ShapeDtypeStruct((32, 2048), F32)),
+        in_specs=[vmem] * 2,
+        out_specs=(vmem, vmem),
+        name="place",
+    )(error.reshape(64, 2048), gradient)
 
 
 def solution(mesh):

time: 184 us -> 153 us (0.83)
  Pallas kernels: 178 us -> 152 us
  local copies, waits for them, and re-layouts: 3.34 us -> 0 us
    pallas_call x1, Pallas kernels: 178 us -> 150 us  [body(): pl.pallas_call(kernel, out_shape=(jax.ShapeDtypeStruct((K, 16, 2048), BF1...]
    unnamed x2 -> x0, local copies, waits for them, and re-layouts: 3.34 us -> none
where the time goes in v2:
time: 153 us
  Pallas kernels  152 us (99%)
    pallas_call x1, Pallas kernels, body(): pl.pallas_call(kernel, out_shape=(jax.ShapeDtypeStruct((K, 16, 2048), BF1...  150 us

profile of v2, /device:TPU:8, one launch (start us, length us, event | category | flops | bytes accessed | tf_op | source)
XLA Modules:
  0.0 152.5 jit_solution(16792073443802849771)
XLA Ops:
  0.6 150.0 %distill.1 = (bf16[4,16,2048]{2,1,0:T(8,128)(2,1)}, f32[32,2048]{1,0:T(8,128)}) custom-call(bf16[2,2,4,16,8192]{4,3,2,1,0:T(8,128)(2,1)} %bitcast.5, bf16[2,2,4,16,8192]{4,3,2,1,0:T(8,128)(2,1)} %bitcast.6, f32[1,2048]{1,0:T(1,128)} %bitcast.9, bf16[32,2048]{1,0:T(8,128)(2,1)} %proj.1, bf16[2,2,4,16,2048]{4,3,2,1,0:T(8,128)(2,1)} %bitcast.7), custom_call_target="tpu_custom_call" | custom-call | tf_op jit(solution)/shard_map/distill/pallas_call | solution.py:368
  150.7 1.8 %place.1 = (bf16[64,2048]{1,0:T(8,128)(2,1)}, f32[32,2048]{1,0:T(8,128)}) custom-call(bf16[64,2048]{1,0:T(8,128)(2,1)} %bitcast.8, f32[32,2048]{1,0:T(8,128)} %get-tuple-element.5.gradient), custom_call_target="tpu_custom_call" | custom-call | tf_op jit(solution)/shard_map/place/pallas_call | solution.py:411

commit v3 on v2

v3 whole, which is shorter than its diff:
```python
import jax
import jax.numpy as jnp
from jax import lax
from jax.experimental import pallas as pl
from jax.experimental.pallas import tpu as pltpu
from jax.sharding import PartitionSpec as P

MESH_ID = pl.DeviceIdType.MESH
F32 = jnp.float32
BF16 = jnp.bfloat16
EPS = 1e-05
DT = 8192
NX_, NY_, NZL, NZ = 4, 4, 4, 8
K = 4
TILE = 512


def dot_nt(a, b):
    return lax.dot_general(a, b, (((1,), (1,)), ((), ())), preferred_element_type=F32)


def dot_tn(a, b):
    return lax.dot_general(a, b, (((0,), (0,)), ((), ())), preferred_element_type=F32)


def kernel(
    tp, res, gain, proj, stu, out_e, out_g,
    t_own, t_rem, r_own, hid, z_out, z_in, gains, sq_out, sq_in, n_out, norm,
    w, st_raw, st_out, st_in, pp, pp_out, pp_in, q_out, q_in, err, e_in, grad, g_out, g_in, f_out, f_in, f_own,
    e_all, g_all,
    send_sem, recv_sem, local_sem, ready,
):
    dp = lax.axis_index("dp")
    tensor = lax.axis_index("tensor")
    x = lax.rem(dp, NX_)
    y = lax.rem(dp // NX_, NY_)
    zl = dp // (NX_ * NY_)
    zh = tensor // 2
    c = lax.rem(tensor, 2)
    z = zh * NZL + zl
    other = 1 - c

    def device(dx=0, dy=0, dz=0, dc=0):
        x1 = lax.rem(x + dx, NX_)
        y1 = lax.rem(y + dy, NY_)
        z1 = lax.rem(z + dz, NZ)
        c1 = lax.rem(c + dc, 2)
        return (lax.rem(z1, NZL) * (NX_ * NY_) + y1 * NX_ + x1, (z1 // NZL) * 2 + c1)

    counts = {"recv": 0, "local": 0}
    sends = {}

    def remote(kind, whole, *pairs, start=True):
        i = counts["recv"]
        counts["recv"] += 1
        j = sends.setdefault(kind, len(sends))
        copies = [
            pltpu.make_async_remote_copy(
                src, dst, send_sem.at[j], recv_sem.at[i], device_id=device(**offset), device_id_type=MESH_ID
            )
            for src, dst, offset in pairs
        ]
        if start:
            for copy in copies:
                copy.start()
        return pltpu.make_async_copy(whole, whole, recv_sem.at[i]), copies

    def local(whole, *pairs):
        i = counts["local"]
        counts["local"] += 1
        for src, dst in pairs:
            pltpu.make_async_copy(src, dst, local_sem.at[i]).start()
        return pltpu.make_async_copy(whole, whole, local_sem.at[i])

    def arrived(group):
        group[0].wait()

    def cols(index, width):
        return pl.ds(pl.multiple_of(index * width, width), width)

    half = [pl.ds(h * 2048, 2048) for h in range(2)]
    mine = [cols(2 * h + c, 2048) for h in range(2)]
    theirs = [cols(2 * h + other, 2048) for h in range(2)]
    early = [
        local(t_own.at[0, :, k], *[(tp.at[1 - zh, :, k, :, mine[h]], t_own.at[0, :, k, :, half[h]]) for h in range(2)])
        for k in range(K)
    ]
    late = [local(t_own.at[1], *[(tp.at[zh, :, :, :, mine[h]], t_own.at[1, :, :, :, half[h]]) for h in range(2)])]
    late += [local(r_own, *[(res.at[zh, :, :, :, mine[h]], r_own.at[:, :, :, half[h]]) for h in range(2)])]
    late_gain = local(gains.at[0], (gain, gains.at[zh]))
    late_student = local(st_raw, (stu.at[zh, c], st_raw))
    own_rows = w.at[z, pl.ds(pl.multiple_of(x * 32, 32), 32)]
    late_w = local(own_rows, (proj.at[:, cols(x, TILE)], own_rows))

    partners = [dict(dc=1)]
    partners += [dict(dz=d) for d in range(1, NZ)]
    partners += [dict(dx=d) for d in range(1, NX_)]
    partners += [dict(dy=d) for d in range(1, NY_)]
    barrier = pltpu.get_barrier_semaphore()
    for offset in partners:
        pl.semaphore_signal(barrier, inc=1, device_id=device(**offset), device_id_type=MESH_ID)
    pl.semaphore_wait(barrier, len(partners))

    gain_in = remote("gain", gains.at[0], (gain, gains.at[zh], dict(dz=4)))
    early_in = [
        remote(
            "early", t_rem.at[0, :, k],
            *[(tp.at[1 - zh, :, k, :, theirs[h]], t_rem.at[0, :, k, :, half[h]], dict(dc=1)) for h in range(2)],
        )
        for k in range(K)
    ]
    late_in = remote(
        "late", t_rem.at[1],
        *[(tp.at[zh, :, :, :, theirs[h]], t_rem.at[1, :, :, :, half[h]], dict(dc=1)) for h in range(2)],
    )
    w_x = remote(
        "w_x", w.at[0, 0:96],
        *[(proj.at[:, cols(lax.rem(x + d, NX_), TILE)], own_rows, dict(dx=d)) for d in range(1, NX_)],
    )

    pieces = [(k, part, h) for k in range(K) for part in range(2) for h in range(2)]
    z_copy = [
        remote(
            "z", z_in.at[k],
            *[
                (z_out.at[k, part, :, half[h]], z_in.at[k, part, :, half[h]], dict(dz=4))
                for part in range(2) for h in range(2)
            ],
            start=False,
        )
        for k in range(K)
    ]

    def send_pieces(first, last):
        for k, part, h in pieces[first:last]:
            z_copy[k][1][2 * part + h].start()

    def ring_step(s):
        right = lax.rem(z + NZ - (s - 1), NZ)
        left = lax.rem(z + (s - 1), NZ)
        return remote(
            "ring", w.at[0:2],
            (w.at[right], w.at[right], dict(dz=1)), (w.at[left], w.at[left], dict(dz=NZ - 1)),
        )

    def pair_sum(k):
        early[k].wait()
        arrived(early_in[k])

        @pl.loop(0, 4096 // TILE)
        def _(t):
            at = cols(t, TILE)
            pair = t_own[0, :, k, :, at].astype(F32) + t_rem[0, :, k, :, at].astype(F32)
            z_out[k, :, :, at] = pair.astype(BF16)

    pair_sum(0)
    send_pieces(0, 2)
    for k in range(1, K):
        pair_sum(k)
    late_w.wait()
    arrived(w_x)
    ring = ring_step(1)
    far = remote("far", w.at[z], (w.at[z], w.at[z], dict(dz=4)))

    for copy in late:
        copy.wait()
    arrived(late_in)
    for k in range(K):

        @pl.loop(0, 4096 // TILE)
        def _(t, k=k):
            at = cols(t, TILE)
            hid[k, :, :, at] = (
                r_own[:, k, :, at].astype(F32) + t_own[1, :, k, :, at].astype(F32) + t_rem[1, :, k, :, at].astype(F32)
            )

    late_student.wait()
    for y1 in range(NY_):
        for b in range(NZL):
            st_out[y1, :, :, b * 128 : (b + 1) * 128] = st_raw[:, :, b * 512 + y1 * 128 : b * 512 + (y1 + 1) * 128]
    st_own = local(st_in.at[y], (st_out.at[y], st_in.at[y]))
    st_copy = remote(
        "student", st_in.at[0:3], *[(st_out.at[lax.rem(y + d, NY_)], st_in.at[y], dict(dy=d)) for d in range(1, NY_)]
    )

    arrived(ring)
    ring = ring_step(2)
    send_pieces(2, 3)
    late_gain.wait()
    arrived(gain_in)

    x_own, x_copy, y_copy, p_copy, q_copy, e_copy, s_copy = {}, {}, {}, {}, {}, {}, {}

    def normalise(k):
        arrived(z_copy[k])

        def add(t, total):
            at = cols(t, TILE)
            value = hid[k, :, :, at] + z_in[k, :, :, at].astype(F32)
            hid[k, :, :, at] = value
            square = value * value
            for b in range(TILE // 128):
                total = total + square[:, :, b * 128 : (b + 1) * 128]
            return total

        sq_out[k] = lax.fori_loop(0, 4096 // TILE, add, jnp.zeros((2, 16, 128), F32))
        arrived(remote("square", sq_in.at[k], (sq_out.at[k], sq_in.at[k], dict(dc=1))))
        whole = jnp.sum(sq_out[k] + sq_in[k], axis=-1, keepdims=True)
        inv = lax.rsqrt(whole / DT + EPS)
        for h in range(2):

            @pl.loop(0, NX_)
            def _(x1, h=h):
                at = pl.ds(pl.multiple_of(h * 2048 + x1 * TILE, TILE), TILE)
                g = gains[h, :, cols(x1, TILE)]
                n_out[k, x1, :, :, h * TILE : (h + 1) * TILE] = (hid[k, :, :, at] * inv * g[None]).astype(BF16)

        own = norm.at[k, y, x]
        x_own[k] = local(own, (n_out.at[k, x], own))
        x_copy[k] = remote(
            "x", n_out.at[k, 0:3], *[(n_out.at[k, lax.rem(x + d, NX_)], own, dict(dx=d)) for d in range(1, NX_)]
        )

    def gather_y(k):
        x_own[k].wait()
        arrived(x_copy[k])
        block = norm.at[k, y]
        y_copy[k] = remote("y", norm.at[k, 0:2], *[(block, block, dict(dy=d)) for d in (1, NY_ - 1)])

    def forward_y(k):
        arrived(y_copy[k])
        blocks = [
            (norm.at[k, lax.rem(y + NY_ - d, NY_), 2 * i : 2 * i + 2], dict(dy=d)) for i, d in enumerate((1, NY_ - 1))
        ]
        y_copy[k] = remote("forward", norm.at[k, 0], *[(block, block, offset) for block, offset in blocks])

    def product(k, half, n):
        total = None
        for h in range(2):
            rows = norm[k, :, :, half, :, h * TILE : (h + 1) * TILE].reshape(256, TILE)
            weights = w[4 * h + 2 * n : 4 * h + 2 * n + 2].reshape(256, TILE)
            part = dot_nt(rows, weights)
            total = part if total is None else total + part
        return total.reshape(NY_, NX_, 16, 256)

    def project(k):
        arrived(y_copy[k])
        for own in (False, True):
            for n in range(2):
                total = product(k, c if own else other, n)
                if own:
                    pp[k % 2, :, :, :, n * 256 : (n + 1) * 256] = total
                else:
                    pp_out[k, :, :, :, n * 256 : (n + 1) * 256] = total.astype(BF16)
            if not own:
                p_copy[k] = remote("pair", pp_in.at[k], (pp_out.at[k], pp_in.at[k], dict(dc=1)))

    def pair_up(k):
        arrived(p_copy[k])

        @pl.loop(0, NY_)
        def _(y1):
            total = pp[k % 2, y1] + pp_in[k, y1].astype(F32)
            pp[k % 2, y1] = total
            q_out[k, y1] = total.astype(BF16)

        q_copy[k] = remote(
            "q", q_in.at[k, 0:3],
            *[(q_out.at[k, :, lax.rem(x + d, NX_)], q_in.at[k, x], dict(dx=d)) for d in range(1, NX_)],
        )

    def subtract(k):
        arrived(q_copy[k])

        @pl.loop(0, NY_)
        def _(y1):
            total = pp[k % 2, y1, x]
            for d in range(1, NX_):
                total = total + q_in[k, lax.rem(x + d, NX_), y1].astype(F32)
            err[k, y1, x, c] = (total - st_in[y1, k].astype(F32)).astype(BF16)

        own = err.at[k, :, x, c]
        e_copy[k] = remote("error", q_in.at[k, 0:3], *[(own, own, dict(dx=d)) for d in range(1, NX_)])
        e_in[y, k] = err[k, y, x, c]
        for i, d in enumerate(range(1, NY_)):
            o_copy[1][3 * k + i].start()

    def share(k):
        arrived(e_copy[k])
        rows = err.at[k, :, :, c]
        s_copy[k] = remote("share", pp_in.at[k], (rows, rows, dict(dc=1)))

    def accumulate(k):
        arrived(s_copy[k])
        e = err[k].reshape(512, 512)
        for h in range(2):
            n = norm[k, :, :, :, :, h * TILE : (h + 1) * TILE].reshape(512, TILE)
            part = dot_tn(e, n).reshape(NZL, 128, TILE)
            grad[h] = part if k == 0 else grad[h] + part

    arrived(st_copy)
    st_own.wait()
    o_copy = remote(
        "out", e_in.at[0:3],
        *[
            (err.at[k, lax.rem(y + d, NY_), x, c], e_in.at[y, k], dict(dy=d))
            for k in range(K) for d in range(1, NY_)
        ],
        start=False,
    )

    arrived(ring)
    ring = ring_step(3)
    send_pieces(3, 4)
    arrived(ring)
    arrived(far)
    send_pieces(4, 6)
    pl.semaphore_signal(ready.at[0], inc=1, device_id=device(dc=1), device_id_type=MESH_ID)
    pl.semaphore_wait(ready.at[0], 1)
    for d in range(1, NZ):
        pl.semaphore_signal(ready.at[1], inc=1, device_id=device(dz=d), device_id_type=MESH_ID)
    normalise(0)
    pl.semaphore_wait(ready.at[1], NZ - 1)
    send_pieces(6, len(pieces))
    gather_y(0)
    for stage, k in (
        (normalise, 1), (forward_y, 0), (gather_y, 1), (project, 0),
        (normalise, 2), (pair_up, 0), (forward_y, 1), (gather_y, 2), (project, 1), (subtract, 0),
        (normalise, 3), (pair_up, 1), (forward_y, 2), (gather_y, 3), (share, 0), (project, 2), (subtract, 1),
        (pair_up, 2), (accumulate, 0), (forward_y, 3), (share, 1), (subtract, 2), (project, 3), (accumulate, 1),
        (pair_up, 3), (share, 2), (subtract, 3), (accumulate, 2), (share, 3), (accumulate, 3),
    ):
        stage(k)

    def hops(sub, way):
        return 4 if sub % 2 == way else 3

    g_copy = {}
    for s in range(1, 5):
        for sub in range(4):
            for way in range(2):
                n = hops(sub, way)
                if s > n:
                    continue
                far = n + 1 - s
                d = lax.rem(z + (far if way == 0 else NZ - far), NZ)
                total = grad[d // NZL, lax.rem(d, NZL), sub * 32 : (sub + 1) * 32]
                if s > 1:
                    arrived(g_copy[sub, way, s - 1])
                    total = total + g_in[sub, way, s - 2].astype(F32)
                g_out[sub, way, s - 1] = total.astype(BF16)
                step = g_in.at[sub, way, s - 1]
                offset = dict(dz=1 if way == 0 else NZ - 1)
                g_copy[sub, way, s] = remote("sum", step, (g_out.at[sub, way, s - 1], step, offset))
        if s == 1:
            arrived(o_copy)
            for y1 in range(NY_):
                for b in range(NZL):
                    e_all[:, :, b * 512 + y1 * 128 : b * 512 + (y1 + 1) * 128] = e_in[y1, :, :, b * 128 : (b + 1) * 128]
            e_done = local(e_all, (e_all, out_e))
    for x1 in range(NX_):
        total = grad[zh, zl, x1 * 32 : (x1 + 1) * 32]
        for way in range(2):
            n = hops(x1, way)
            arrived(g_copy[x1, way, n])
            total = total + g_in[x1, way, n - 1].astype(F32)
        total = total * (1.0 / 256)
        f_out[x1] = total.astype(BF16)
        f_own[x1] = total
    f_copy = remote("final", f_in.at[0:3], *[(f_out.at[lax.rem(x + d, NX_)], f_in.at[x], dict(dx=d)) for d in (1, 3, 2)])
    g_all[:, cols(x, TILE)] = f_own[x]
    arrived(f_copy)
    for d in range(1, NX_):
        x1 = lax.rem(x + d, NX_)
        g_all[:, cols(x1, TILE)] = f_in[x1].astype(F32)
    done = local(g_all, (g_all, out_g))
    e_done.wait()
    done.wait()
    sent = {
        "gain": gains.at[0], "early": t_rem.at[0], "late": t_rem.at[1], "w_x": w.at[0, 0:96], "ring": w.at[0:6],
        "far": w.at[0], "student": st_in.at[0:3], "z": z_in, "square": sq_in, "x": n_out.at[:, 0:3],
        "y": norm.at[0:2], "forward": norm.at[0], "pair": pp_in, "q": q_in.at[:, 0:3], "error": q_in.at[:, 0:3],
        "share": pp_in, "out": e_in.at[0:3], "sum": w.at[0:7], "final": f_in.at[0:3],
    }
    for kind, j in sends.items():
        pltpu.make_async_copy(sent[kind], sent[kind], send_sem.at[j]).wait()


def place(error, gradient, out_e, out_g):
    out_e[...] = error[...]
    out_g[...] = gradient[...]


def body(teacher_partial, teacher_resid, norm_gain, projector, student_hidden):
    tp = teacher_partial.reshape(2, 2, K, 16, DT)
    res = teacher_resid.reshape(2, 2, K, 16, DT)
    stu = student_hidden.reshape(2, 2, K, 16, 2048)
    hbm = pl.BlockSpec(memory_space=pl.ANY)
    vmem = pl.BlockSpec(memory_space=pltpu.VMEM)
    error, gradient = pl.pallas_call(
        kernel,
        out_shape=(jax.ShapeDtypeStruct((K, 16, 2048), BF16), jax.ShapeDtypeStruct((32, 2048), F32)),
        in_specs=[hbm] * 5,
        out_specs=(hbm, hbm),
        scratch_shapes=[
            pltpu.VMEM((2, 2, K, 16, 4096), BF16),
            pltpu.VMEM((2, 2, K, 16, 4096), BF16),
            pltpu.VMEM((2, K, 16, 4096), BF16),
            pltpu.VMEM((K, 2, 16, 4096), F32),
            pltpu.VMEM((K, 2, 16, 4096), BF16),
            pltpu.VMEM((K, 2, 16, 4096), BF16),
            pltpu.VMEM((2, 1, 2048), F32),
            pltpu.VMEM((K, 2, 16, 128), F32),
            pltpu.VMEM((K, 2, 16, 128), F32),
            pltpu.VMEM((K, 4, 2, 16, 1024), BF16),
            pltpu.VMEM((K, 4, 4, 2, 16, 1024), BF16),
            pltpu.VMEM((8, 128, 512), BF16),
            pltpu.VMEM((K, 16, 2048), BF16),
            pltpu.VMEM((4, K, 16, 512), BF16),
            pltpu.VMEM((4, K, 16, 512), BF16),
            pltpu.VMEM((2, 4, 4, 16, 512), F32),
            pltpu.VMEM((K, 4, 4, 16, 512), BF16),
            pltpu.VMEM((K, 4, 4, 16, 512), BF16),
            pltpu.VMEM((K, 4, 4, 16, 512), BF16),
            pltpu.VMEM((K, 4, 4, 16, 512), BF16),
            pltpu.VMEM((K, 4, 4, 2, 16, 512), BF16),
            pltpu.VMEM((4, K, 16, 512), BF16),
            pltpu.VMEM((2, 4, 128, 512), F32),
            pltpu.VMEM((4, 2, 4, 32, 512), BF16),
            pltpu.VMEM((4, 2, 4, 32, 512), BF16),
            pltpu.VMEM((4, 32, 512), BF16),
            pltpu.VMEM((4, 32, 512), BF16),
            pltpu.VMEM((4, 32, 512), F32),
            pltpu.VMEM((K, 16, 2048), BF16),
            pltpu.VMEM((32, 2048), F32),
            pltpu.SemaphoreType.DMA((19,)),
            pltpu.SemaphoreType.DMA((78,)),
            pltpu.SemaphoreType.DMA((16,)),
            pltpu.SemaphoreType.REGULAR((2,)),
        ],
        compiler_params=pltpu.CompilerParams(
            collective_id=0, has_side_effects=True, vmem_limit_bytes=56 << 20
        ),
        name="distill",
    )(tp, res, norm_gain.reshape(1, -1), projector, stu)
    return pl.pallas_call(
        place,
        out_shape=(jax.ShapeDtypeStruct((64, 2048), BF16), jax.ShapeDtypeStruct((32, 2048), F32)),
        in_specs=[vmem] * 2,
        out_specs=(vmem, vmem),
        name="place",
    )(error.reshape(64, 2048), gradient)


def solution(mesh):
    placed = (P("tensor", "dp", None), P("dp", None), P("tensor"), P("dp", "tensor"), P("dp", None))
    return jax.shard_map(
        body,
        mesh=mesh,
        in_specs=placed,
        out_specs=(P(("dp", "tensor"), None), P("dp", "tensor")),
        check_vma=False,
    )
```

time: 153 us -> 140 us (0.915)
  Pallas kernels: 152 us -> 139 us
    pallas_call x1, Pallas kernels: 150 us -> 137 us  [body(): pl.pallas_call(kernel, out_shape=(jax.ShapeDtypeStruct((K, 16, 2048), BF1...]
where the time goes in v3:
time: 140 us
  Pallas kernels  139 us (99%)
    pallas_call x1, Pallas kernels, body(): pl.pallas_call(kernel, out_shape=(jax.ShapeDtypeStruct((K, 16, 2048), BF1...  137 us

profile of v3, /device:TPU:8, one launch (start us, length us, event | category | flops | bytes accessed | tf_op | source)
XLA Modules:
  0.0 139.7 jit_solution(11650594984178767688)
XLA Ops:
  0.6 137.3 %distill.1 = (bf16[4,16,2048]{2,1,0:T(8,128)(2,1)}, f32[32,2048]{1,0:T(8,128)}) custom-call(bf16[2,2,4,16,8192]{4,3,2,1,0:T(8,128)(2,1)} %bitcast.5, bf16[2,2,4,16,8192]{4,3,2,1,0:T(8,128)(2,1)} %bitcast.6, f32[1,2048]{1,0:T(1,128)} %bitcast.9, bf16[32,2048]{1,0:T(8,128)(2,1)} %proj.1, bf16[2,2,4,16,2048]{4,3,2,1,0:T(8,128)(2,1)} %bitcast.7), custom_call_target="tpu_custom_call" | custom-call | tf_op jit(solution)/shard_map/distill/pallas_call | solution.py:400
  137.9 1.8 %place.1 = (bf16[64,2048]{1,0:T(8,128)(2,1)}, f32[32,2048]{1,0:T(8,128)}) custom-call(bf16[64,2048]{1,0:T(8,128)(2,1)} %bitcast.8, f32[32,2048]{1,0:T(8,128)} %get-tuple-element.5.gradient), custom_call_target="tpu_custom_call" | custom-call | tf_op jit(solution)/shard_map/place/pallas_call | solution.py:446

commit v4 on v3

--- a/solution.py
+++ b/solution.py
@@ -160,7 +160,7 @@
     late_w.wait()
     arrived(w_x)
     ring = ring_step(1)
-    far = remote("far", w.at[z], (w.at[z], w.at[z], dict(dz=4)))
+    send_pieces(2, 3)
 
     for copy in late:
         copy.wait()
@@ -185,7 +185,7 @@
 
     arrived(ring)
     ring = ring_step(2)
-    send_pieces(2, 3)
+    send_pieces(3, 4)
     late_gain.wait()
     arrived(gain_in)
 
@@ -311,26 +311,33 @@
 
     arrived(ring)
     ring = ring_step(3)
-    send_pieces(3, 4)
+    send_pieces(4, 5)
     arrived(ring)
-    arrived(far)
-    send_pieces(4, 6)
+    right = w.at[lax.rem(z + NZ - 3, NZ), 0:64]
+    left = w.at[lax.rem(z + 3, NZ), 64:128]
+    ring = remote("far", w.at[0], (right, right, dict(dz=1)), (left, left, dict(dz=NZ - 1)))
+    send_pieces(5, 6)
+    normalise(0)
+    arrived(ring)
+    send_pieces(6, 8)
     pl.semaphore_signal(ready.at[0], inc=1, device_id=device(dc=1), device_id_type=MESH_ID)
     pl.semaphore_wait(ready.at[0], 1)
     for d in range(1, NZ):
         pl.semaphore_signal(ready.at[1], inc=1, device_id=device(dz=d), device_id_type=MESH_ID)
-    normalise(0)
+    gather_y(0)
     pl.semaphore_wait(ready.at[1], NZ - 1)
-    send_pieces(6, len(pieces))
-    gather_y(0)
+    send_pieces(8, 10)
+    paced = {(normalise, 1): [(10, 12)], (gather_y, 1): [(12, 14)], (normalise, 2): [(14, 16)]}
     for stage, k in (
         (normalise, 1), (forward_y, 0), (gather_y, 1), (project, 0),
-        (normalise, 2), (pair_up, 0), (forward_y, 1), (gather_y, 2), (project, 1), (subtract, 0),
-        (normalise, 3), (pair_up, 1), (forward_y, 2), (gather_y, 3), (share, 0), (project, 2), (subtract, 1),
-        (pair_up, 2), (accumulate, 0), (forward_y, 3), (share, 1), (subtract, 2), (project, 3), (accumulate, 1),
-        (pair_up, 3), (share, 2), (subtract, 3), (accumulate, 2), (share, 3), (accumulate, 3),
+        (normalise, 2), (forward_y, 1), (gather_y, 2), (pair_up, 0), (project, 1),
+        (normalise, 3), (subtract, 0), (forward_y, 2), (gather_y, 3), (pair_up, 1), (project, 2), (share, 0),
+        (subtract, 1), (accumulate, 0), (pair_up, 2), (forward_y, 3), (share, 1), (project, 3), (subtract, 2),
+        (pair_up, 3), (accumulate, 1), (share, 2), (subtract, 3), (accumulate, 2), (share, 3), (accumulate, 3),
     ):
         stage(k)
+        for first, last in paced.get((stage, k), ()):
+            send_pieces(first, last)
 
     def hops(sub, way):
         return 4 if sub % 2 == way else 3

time: 140 us -> 133 us (0.950)
  Pallas kernels: 139 us -> 132 us
    pallas_call x1, Pallas kernels: 137 us -> 131 us  [body(): pl.pallas_call(kernel, out_shape=(jax.ShapeDtypeStruct((K, 16, 2048), BF1...]
where the time goes in v4:
time: 133 us
  Pallas kernels  132 us (99%)
    pallas_call x1, Pallas kernels, body(): pl.pallas_call(kernel, out_shape=(jax.ShapeDtypeStruct((K, 16, 2048), BF1...  131 us

profile of v4, /device:TPU:8, one launch (start us, length us, event | category | flops | bytes accessed | tf_op | source)
XLA Modules:
  0.0 133.1 jit_solution(4762136299364801287)
XLA Ops:
  0.6 130.6 %distill.1 = (bf16[4,16,2048]{2,1,0:T(8,128)(2,1)}, f32[32,2048]{1,0:T(8,128)}) custom-call(bf16[2,2,4,16,8192]{4,3,2,1,0:T(8,128)(2,1)} %bitcast.5, bf16[2,2,4,16,8192]{4,3,2,1,0:T(8,128)(2,1)} %bitcast.6, f32[1,2048]{1,0:T(1,128)} %bitcast.9, bf16[32,2048]{1,0:T(8,128)(2,1)} %proj.1, bf16[2,2,4,16,2048]{4,3,2,1,0:T(8,128)(2,1)} %bitcast.7), custom_call_target="tpu_custom_call" | custom-call | tf_op jit(solution)/shard_map/distill/pallas_call | solution.py:407
  131.2 1.8 %place.1 = (bf16[64,2048]{1,0:T(8,128)(2,1)}, f32[32,2048]{1,0:T(8,128)}) custom-call(bf16[64,2048]{1,0:T(8,128)(2,1)} %bitcast.8, f32[32,2048]{1,0:T(8,128)} %get-tuple-element.5.gradient), custom_call_target="tpu_custom_call" | custom-call | tf_op jit(solution)/shard_map/place/pallas_call | solution.py:453

commit v5 on v4

--- a/solution.py
+++ b/solution.py
@@ -102,6 +102,10 @@
     pl.semaphore_wait(barrier, len(partners))
 
     gain_in = remote("gain", gains.at[0], (gain, gains.at[zh], dict(dz=4)))
+    w_x = remote(
+        "w_x", w.at[0, 0:96],
+        *[(proj.at[:, cols(lax.rem(x + d, NX_), TILE)], own_rows, dict(dx=d)) for d in range(1, NX_)],
+    )
     early_in = [
         remote(
             "early", t_rem.at[0, :, k],
@@ -113,11 +117,6 @@
         "late", t_rem.at[1],
         *[(tp.at[zh, :, :, :, theirs[h]], t_rem.at[1, :, :, :, half[h]], dict(dc=1)) for h in range(2)],
     )
-    w_x = remote(
-        "w_x", w.at[0, 0:96],
-        *[(proj.at[:, cols(lax.rem(x + d, NX_), TILE)], own_rows, dict(dx=d)) for d in range(1, NX_)],
-    )
-
     pieces = [(k, part, h) for k in range(K) for part in range(2) for h in range(2)]
     z_copy = [
         remote(
@@ -154,13 +153,13 @@
             z_out[k, :, :, at] = pair.astype(BF16)
 
     pair_sum(0)
-    send_pieces(0, 2)
+    send_pieces(0, 1)
     for k in range(1, K):
         pair_sum(k)
     late_w.wait()
     arrived(w_x)
     ring = ring_step(1)
-    send_pieces(2, 3)
+    send_pieces(1, 3)
 
     for copy in late:
         copy.wait()

time: 133 us -> 136 us (1.023); the launches traced: 133 us -> 134 us
  no operation moved by 1% of the time
where the time goes in v5:
time: 136 us; the launch traced here: 134 us
  Pallas kernels  133 us (98%)
    pallas_call x1, Pallas kernels, body(): pl.pallas_call(kernel, out_shape=(jax.ShapeDtypeStruct((K, 16, 2048), BF1...  132 us

profile of v5, /device:TPU:8, one launch (start us, length us, event | category | flops | bytes accessed | tf_op | source)
XLA Modules:
  0.0 134.1 jit_solution(17875174475780100483)
XLA Ops:
  0.6 131.6 %distill.1 = (bf16[4,16,2048]{2,1,0:T(8,128)(2,1)}, f32[32,2048]{1,0:T(8,128)}) custom-call(bf16[2,2,4,16,8192]{4,3,2,1,0:T(8,128)(2,1)} %bitcast.5, bf16[2,2,4,16,8192]{4,3,2,1,0:T(8,128)(2,1)} %bitcast.6, f32[1,2048]{1,0:T(1,128)} %bitcast.9, bf16[32,2048]{1,0:T(8,128)(2,1)} %proj.1, bf16[2,2,4,16,2048]{4,3,2,1,0:T(8,128)(2,1)} %bitcast.7), custom_call_target="tpu_custom_call" | custom-call | tf_op jit(solution)/shard_map/distill/pallas_call | solution.py:406
  132.2 1.8 %place.1 = (bf16[64,2048]{1,0:T(8,128)(2,1)}, f32[32,2048]{1,0:T(8,128)}) custom-call(bf16[64,2048]{1,0:T(8,128)(2,1)} %bitcast.8, f32[32,2048]{1,0:T(8,128)} %get-tuple-element.5.gradient), custom_call_target="tpu_custom_call" | custom-call | tf_op jit(solution)/shard_map/place/pallas_call | solution.py:452
